TPU v7x, 32 devices: a whole 2x2x4 slice. The times are simulated.
32 devices in a mesh: groups: 2 (over y), chan: 4 (over z), space: 2 (over x), dp: 2 (over core).
Axes of the slice: x: 2, y: 2, z: 4, core: 2. Of those that a mesh axis runs over, the one named last changes fastest.
Arguments:
- inputs: bfloat16 [4, 4, 16, 16, 512], P(('groups', 'dp'), 'space', None, None, 'chan'), parts along dimension 0, may hold values from -6 to 6
- weights: bfloat16 [27, 512, 512], P(None, 'chan'), may hold values from -0.0625 to 0.0625
- bias: float32 [512], P('chan'), may hold values from -3 to 3
- upstream: bfloat16 [4, 4, 16, 16, 512], P(('groups', 'dp'), 'space', None, None, 'chan'), parts along dimension 0, may hold values from -6 to 6
Outputs:
- activated: bfloat16 [4, 4, 16, 16, 512], P(('groups', 'dp'), 'space', None, None, 'chan'), parts along dimension 0
- grad_inputs: bfloat16 [4, 4, 16, 16, 512], P(('groups', 'dp'), 'space', None, None, 'chan'), parts along dimension 0
- grad_weights: float32 [54, 512, 512], P('groups', 'chan', ('space', 'dp')), parts along dimension 0
There are 2 independent parts, one for each index of `groups`. A program takes and returns all parts, laid end to end along the dimension named above; an argument that names none is the same for every part. Nothing has to cross between parts.
All inputs are finite; a program needn't handle non-finite values.
Results may differ from a plain program's by a relative error of at most 0.0049.
Values may be sent and summed in bfloat16 or wider, within the bound.
A program may use at most 64 MiB of HBM per device.

v0:
```python
import math

import jax
import jax.numpy as jnp
from jax import lax
from jax.sharding import PartitionSpec as P

tap_offsets = [(a, b, c) for a in (-1, 0, 1) for b in (-1, 0, 1) for c in (-1, 0, 1)]


def extended(array, sides, width):
    for axis, dim in sides:
        size, length = (lax.axis_size(axis), array.shape[dim])
        up = [(i, (i + 1) % size) for i in range(size - 1)]
        down = [(j, i) for i, j in up]
        last = lax.slice_in_dim(array, length - width, length, axis=dim)
        leading = lax.slice_in_dim(array, 0, width, axis=dim)
        before = lax.ppermute(last, axis, up)
        after = lax.ppermute(leading, axis, down)
        array = jnp.concatenate([before, array, after], axis=dim)
    return array


def spatial_pad(volume):
    return jnp.pad(volume, ((0, 0), (0, 0), (1, 1), (1, 1), (0, 0)))


def tap_slice(volume, a, b, c, width_x, width_y, width_z):
    return volume[:, 1 + a : 1 + a + width_x, 1 + b : 1 + b + width_y, 1 + c : 1 + c + width_z]


def local(inputs, weights, bias, upstream):
    batch_size, width_x, width_y, width_z, group_width = inputs.shape
    voxels = batch_size * width_x * width_y * width_z
    tap_count = weights.shape[0]
    outputs_all = weights.shape[2]
    bordered = spatial_pad(extended(inputs, (("space", 1),), 1))
    stacked = jnp.concatenate(
        [
            tap_slice(bordered, a, b, c, width_x, width_y, width_z).reshape(voxels, group_width)
            for a, b, c in tap_offsets
        ],
        axis=1,
    )
    flat_weights = weights.reshape(tap_count * group_width, outputs_all)
    out_share = outputs_all // lax.axis_size("chan")
    summed = lax.psum_scatter(
        lax.dot_general(
            flat_weights, stacked, (((0,), (1,)), ((), ())), preferred_element_type=jnp.float32
        ),
        "chan",
        scatter_dimension=0,
        tiled=True,
    ).T
    preact = summed + bias[None, :]
    gate_value = jax.nn.sigmoid(preact)
    activated = (
        (preact * gate_value)
        .astype(jnp.bfloat16)
        .reshape(batch_size, width_x, width_y, width_z, out_share)
    )
    grad_flat = (
        upstream.reshape(voxels, out_share).astype(jnp.float32)
        * gate_value
        * (1.0 + preact * (1.0 - gate_value))
    )
    grad_pre = grad_flat.astype(jnp.bfloat16).reshape(
        batch_size, width_x, width_y, width_z, out_share
    )
    grad_full = lax.all_gather(grad_pre, "chan", axis=4, tiled=True)
    framed = extended(grad_full, (("space", 1),), 1)
    interior = framed[:, 1:-1].reshape(voxels, outputs_all)
    framed_all = spatial_pad(framed)
    padded_shape = framed_all.shape
    projected = lax.dot_general(
        framed_all.reshape(-1, outputs_all),
        flat_weights,
        (((1,), (1,)), ((), ())),
        preferred_element_type=jnp.float32,
    )
    projected = projected.reshape(
        padded_shape[0], padded_shape[1], padded_shape[2], padded_shape[3], tap_count, group_width
    )
    grad_in = jnp.zeros((batch_size, width_x, width_y, width_z, group_width), jnp.float32)
    for k, (a, b, c) in enumerate(tap_offsets):
        grad_in = (
            grad_in
            + projected[
                :, 1 - a : 1 - a + width_x, 1 - b : 1 - b + width_y, 1 - c : 1 - c + width_z, k, :
            ]
        )
    grad_inputs = grad_in.astype(jnp.bfloat16)
    weight_partial = lax.dot_general(
        stacked, interior, (((0,), (0,)), ((), ())), preferred_element_type=jnp.float32
    )
    weight_partial = weight_partial.reshape(tap_count, group_width, outputs_all)
    reduced = lax.psum_scatter(weight_partial, ("space", "dp"), scatter_dimension=2, tiled=True)
    total_voxels = voxels * lax.axis_size("space") * lax.axis_size("dp")
    grad_weights = reduced * (1.0 / math.sqrt(total_voxels))
    return (activated, grad_inputs, grad_weights)


def solution(mesh):
    return jax.shard_map(
        local,
        mesh=mesh,
        in_specs=(
            P(("groups", "dp"), "space", None, None, "chan"),
            P(None, "chan", None),
            P("chan"),
            P(("groups", "dp"), "space", None, None, "chan"),
        ),
        out_specs=(
            P(("groups", "dp"), "space", None, None, "chan"),
            P(("groups", "dp"), "space", None, None, "chan"),
            P("groups", "chan", ("space", "dp")),
        ),
        check_vma=False,
    )
```

profile of v0, /device:TPU:26, one launch (start us, length us, event | category | flops | bytes accessed | tf_op | source)
XLA Modules:
  0.0 209.3 jit_solution(125363186464683135)
XLA Ops:
  7.2 1.7 fusion.69
  8.9 1.3 collective-permute-start
  10.2 5.8 %collective-permute-start.1 = (bf16[1,1,16,16,128]{4,3,2,1,0:T(8,128)(2,1)}, bf16[1,1,16,16,128]{4,3,2,1,0:T(8,128)(2,1)}, u32[]{:S(2)}, u32[]{:S(2)}) collective-permute-start(bf16[1,1,16,16,128]{4,3,2,1,0:T(8,128)(2,1)} %get-tuple-element.34), channel_id=1, source_target_pairs={{2,0},{3,1},{6,4},{7,5},{10,8},{11,9},{14,12},{15,13},{18,16},{19,... | collective-permute-start | bytes 196616 | tf_op jit(solution)/shard_map/ppermute | solution.py:19
  16.0 1.7 copy.20
  17.7 1.1 select_maximum_fusion.3
  19.7 1.5 fusion.67
  21.2 1.6 pad_maximum_fusion
  22.8 1.7 copy.29
  24.5 1.7 copy.11
  26.2 1.7 copy.12
  27.8 1.7 copy.10
  29.5 1.7 copy.9
  31.1 1.7 copy.8
  32.8 1.7 copy.7
  34.5 1.7 copy.33
  36.1 1.7 copy.32
  37.8 1.7 copy.31
  39.4 1.7 copy.30
  41.1 1.7 copy.28
  42.8 1.7 copy.27
  44.4 1.7 copy.26
  46.1 1.7 copy.25
  47.8 1.7 copy.24
  49.4 1.7 copy.23
  51.1 1.7 copy.22
  52.8 1.7 copy.21
  54.4 1.7 copy.19
  56.1 1.7 copy.18
  57.7 1.7 copy.17
  59.4 1.7 copy.16
  61.0 1.7 copy.15
  62.7 1.7 copy.14
  64.4 1.7 copy.13
  79.5 1.9 copy-done.2
  81.4 3.1 %convolution_bitcast_fusion.1 = f32[512,512]{0,1:T(8,128)} fusion(bf16[512,3456]{0,1:T(8,128)(2,1)S(1)} %constant_dynamic-update-slice_fusion, bf16[3456,512]{1,0:T(8,128)(2,1)S(1)} %bitcast.262), kind=kOutput, calls=%fused_computation.21 | convolution fusion | flops 1811939328 | bytes 8126464 | tf_op jit(solution)/shard_map/dot_general | solution.py:48
  84.5 26.7 %reduce-scatter.3.cloned.1.call-done = f32[128,512]{0,1:T(8,128)} async-done(((f32[512,512]{0,1:T(8,128)}), f32[128,512]{0,1:T(8,128)}) %reduce-scatter.3.cloned.1.call-update) | async-done | bytes 262160 | tf_op jit(solution)/shard_map/reduce_scatter | solution.py:47
  111.2 1.8 fusion.56
  113.0 14.4 %all_gather.3 = bf16[1,2,16,16,512]{4,3,2,1,0:T(8,128)(2,1)S(1)} all-gather(bf16[1,2,16,16,128]{4,3,2,1,0:T(8,128)(2,1)S(1)} %bitcast.290), channel_id=1, replica_groups=mesh['groups'=2,'chan'=4,'space'=2,'dp'=2] {'chan'}, dimensions={4}, use_global_device_ids=true | all-gather | bytes 655360 | tf_op jit(solution)/shard_map/all_gather | solution.py:70
  128.2 6.9 %fusion.70 = f32[27,128,512]{2,1,0:T(8,128)} fusion(bf16[27,128,512]{2,1,0:T(8,128)(2,1)} %bitcast.264, bf16[512,512,1]{1,0,2:T(8,128)(2,1)S(1)} %bitcast.263), kind=kOutput, calls=%fused_computation.139 | convolution fusion | flops 1811939328 | bytes 11141120 | tf_op jit(solution)/shard_map/dot_general | solution.py:93
  135.1 1.1 fusion.66
  136.2 1.3 collective-permute-start.2
  137.5 4.6 %collective-permute-start.3 = (bf16[1,1,16,16,512]{4,3,2,1,0:T(8,128)(2,1)S(1)}, bf16[1,1,16,16,512]{4,3,2,1,0:T(8,128)(2,1)S(1)}, u32[]{:S(2)}, u32[]{:S(2)}) collective-permute-start(bf16[1,1,16,16,512]{4,3,2,1,0:T(8,128)(2,1)S(1)} %get-tuple-element.4), channel_id=1, source_target_pairs={{2,0},{3,1},{6,4},{7,5},{10,8},{11,9},{14,12},{15,13},{18,16},{19,... | collective-permute-start | bytes 786440 | tf_op jit(solution)/shard_map/ppermute | solution.py:19
  142.0 2.4 %collective-permute-done.2 = bf16[1,1,16,16,512]{4,3,2,1,0:T(8,128)(2,1)S(1)} collective-permute-done((bf16[1,1,16,16,512]{4,3,2,1,0:T(8,128)(2,1)S(1)}, bf16[1,1,16,16,512]{4,3,2,1,0:T(8,128)(2,1)S(1)}, u32[]{:S(2)}, u32[]{:S(2)}) %collective-permute-start.2) | collective-permute-done | bytes 262176 | tf_op jit(solution)/shard_map/ppermute | solution.py:18
  144.4 1.5 collective-permute-done.3
  145.9 8.2 %convolution_bitcast_fusion = f32[1,4,18,18,27,128]{5,3,4,2,1,0:T(8,128)S(1)} fusion(bf16[27,128,512]{2,1,0:T(8,128)(2,1)S(1)} %copy-done, bf16[1,1,16,16,512]{4,3,2,1,0:T(8,128)(2,1)S(1)} %collective-permute-done.3, bf16[1,2,16,16,512]{4,3,2,1,0:T(8,128)(2,1)} %copy-done.1, bf16[1,1,16,16,512]{4,3,2,1,0:T(8,128)(2,1)S(1)} %collective-permute-done.2), kind=kOutput, calls=%fused_computation | convolution fusion | flops 4599078912 | bytes 22503424 | tf_op jit(solution)/shard_map/dot_general | solution.py:75
  154.1 1.2 fusion.28
  155.3 44.2 %reduce-scatter.5.cloned.1.call-done = f32[27,128,128]{2,1,0:T(8,128)} async-done(((f32[27,128,512]{2,1,0:T(8,128)}), f32[27,128,128]{2,1,0:T(8,128)}) %reduce-scatter.5.cloned.1.call-update) | async-done | bytes 1769488 | tf_op jit(solution)/shard_map/reduce_scatter | solution.py:97
  199.5 2.9 %broadcast_multiply_fusion = f32[27,128,128]{2,1,0:T(8,128)} fusion(f32[27,128,128]{2,1,0:T(8,128)} %reduce-scatter.5.cloned.1.call-done), kind=kLoop, calls=%fused_computation.27 | loop fusion | flops 442368 | bytes 3538944 | tf_op jit(solution)/shard_map/mul | solution.py:99
  (69 shorter events, 14.9 us)
Async XLA Ops:
  7.2 72.3 %copy-start = (bf16[27,128,512]{2,1,0:T(8,128)(2,1)S(1)}, bf16[27,128,512]{2,1,0:T(8,128)(2,1)}, u32[]{:S(2)}) copy-start(bf16[27,128,512]{2,1,0:T(8,128)(2,1)} %param.5) | copy-start | bytes 10616836
  7.2 104.0 %reduce-scatter.3.cloned.1.call-start = ((), (), s32[]{:S(2)}) async-start(), calls=%async_computation.2 | async-start | bytes 1310720 | tf_op jit(solution)/shard_map/reduce_scatter | solution.py:47
  8.9 8.7 %collective-permute-start = (bf16[1,1,16,16,128]{4,3,2,1,0:T(8,128)(2,1)}, bf16[1,1,16,16,128]{4,3,2,1,0:T(8,128)(2,1)}, u32[]{:S(2)}, u32[]{:S(2)}) collective-permute-start(bf16[1,1,16,16,128]{4,3,2,1,0:T(8,128)(2,1)} %get-tuple-element.33), channel_id=1, source_target_pairs={{0,2},{1,3},{4,6},{5,7},{8,10},{9,11},{12,14},{13,15},{16,18},{17,... | collective-permute-start | bytes 196616 | tf_op jit(solution)/shard_map/ppermute | solution.py:18
  10.2 7.5 %collective-permute-start.1 = (bf16[1,1,16,16,128]{4,3,2,1,0:T(8,128)(2,1)}, bf16[1,1,16,16,128]{4,3,2,1,0:T(8,128)(2,1)}, u32[]{:S(2)}, u32[]{:S(2)}) collective-permute-start(bf16[1,1,16,16,128]{4,3,2,1,0:T(8,128)(2,1)} %get-tuple-element.34), channel_id=1, source_target_pairs={{2,0},{3,1},{6,4},{7,5},{10,8},{11,9},{14,12},{15,13},{18,16},{19,... | collective-permute-start | bytes 196616 | tf_op jit(solution)/shard_map/ppermute | solution.py:19
  17.6 3.6 %copy-start.3 = (bf16[1,2,16,16,128]{4,3,2,1,0:T(8,128)(2,1)S(1)}, bf16[1,2,16,16,128]{4,3,2,1,0:T(8,128)(2,1)}, u32[]{:S(2)}) copy-start(bf16[1,2,16,16,128]{4,3,2,1,0:T(8,128)(2,1)} %param.4) | copy-start | bytes 393220
  66.0 13.1 %copy-start.16 = (bf16[512,128]{0,1:T(8,128)(2,1)S(1)}, bf16[512,128]{0,1:T(8,128)(2,1)}, u32[]{:S(2)}) copy-start(bf16[512,128]{0,1:T(8,128)(2,1)} %copy.21) | copy-start | bytes 393220
  66.0 13.1 %copy-start.15 = (bf16[512,128]{0,1:T(8,128)(2,1)S(1)}, bf16[512,128]{0,1:T(8,128)(2,1)}, u32[]{:S(2)}) copy-start(bf16[512,128]{0,1:T(8,128)(2,1)} %copy.22) | copy-start | bytes 393220
  66.0 13.2 %copy-start.14 = (bf16[512,128]{0,1:T(8,128)(2,1)S(1)}, bf16[512,128]{0,1:T(8,128)(2,1)}, u32[]{:S(2)}) copy-start(bf16[512,128]{0,1:T(8,128)(2,1)} %copy.23) | copy-start | bytes 393220
  66.0 13.2 %copy-start.13 = (bf16[512,128]{0,1:T(8,128)(2,1)S(1)}, bf16[512,128]{0,1:T(8,128)(2,1)}, u32[]{:S(2)}) copy-start(bf16[512,128]{0,1:T(8,128)(2,1)} %copy.24) | copy-start | bytes 393220
  66.0 13.2 %copy-start.12 = (bf16[512,128]{0,1:T(8,128)(2,1)S(1)}, bf16[512,128]{0,1:T(8,128)(2,1)}, u32[]{:S(2)}) copy-start(bf16[512,128]{0,1:T(8,128)(2,1)} %copy.25) | copy-start | bytes 393220
  66.0 13.2 %copy-start.11 = (bf16[512,128]{0,1:T(8,128)(2,1)S(1)}, bf16[512,128]{0,1:T(8,128)(2,1)}, u32[]{:S(2)}) copy-start(bf16[512,128]{0,1:T(8,128)(2,1)} %copy.26) | copy-start | bytes 393220
  66.1 13.2 %copy-start.10 = (bf16[512,128]{0,1:T(8,128)(2,1)S(1)}, bf16[512,128]{0,1:T(8,128)(2,1)}, u32[]{:S(2)}) copy-start(bf16[512,128]{0,1:T(8,128)(2,1)} %copy.27) | copy-start | bytes 393220
  66.1 13.3 %copy-start.9 = (bf16[512,128]{0,1:T(8,128)(2,1)S(1)}, bf16[512,128]{0,1:T(8,128)(2,1)}, u32[]{:S(2)}) copy-start(bf16[512,128]{0,1:T(8,128)(2,1)} %copy.28) | copy-start | bytes 393220
  66.1 13.3 %copy-start.4 = (bf16[512,128]{0,1:T(8,128)(2,1)S(1)}, bf16[512,128]{0,1:T(8,128)(2,1)}, u32[]{:S(2)}) copy-start(bf16[512,128]{0,1:T(8,128)(2,1)} %copy.29) | copy-start | bytes 393220
  66.1 13.3 %copy-start.8 = (bf16[512,128]{0,1:T(8,128)(2,1)S(1)}, bf16[512,128]{0,1:T(8,128)(2,1)}, u32[]{:S(2)}) copy-start(bf16[512,128]{0,1:T(8,128)(2,1)} %copy.30) | copy-start | bytes 393220
  66.1 13.3 %copy-start.7 = (bf16[512,128]{0,1:T(8,128)(2,1)S(1)}, bf16[512,128]{0,1:T(8,128)(2,1)}, u32[]{:S(2)}) copy-start(bf16[512,128]{0,1:T(8,128)(2,1)} %copy.31) | copy-start | bytes 393220
  66.1 13.3 %copy-start.6 = (bf16[512,128]{0,1:T(8,128)(2,1)S(1)}, bf16[512,128]{0,1:T(8,128)(2,1)}, u32[]{:S(2)}) copy-start(bf16[512,128]{0,1:T(8,128)(2,1)} %copy.32) | copy-start | bytes 393220
  66.1 13.4 %copy-start.5 = (bf16[512,128]{0,1:T(8,128)(2,1)S(1)}, bf16[512,128]{0,1:T(8,128)(2,1)}, u32[]{:S(2)}) copy-start(bf16[512,128]{0,1:T(8,128)(2,1)} %copy.33) | copy-start | bytes 393220
  79.5 1.9 copy-start.2
  81.4 29.8 %copy-start.17 = (f32[128]{0:T(128)S(1)}, f32[128]{0:T(128)}, u32[]{:S(2)}) copy-start(f32[128]{0:T(128)} %param.6) | copy-start | bytes 1540
  84.5 115.1 %reduce-scatter.5.cloned.1.call-start = ((), (), s32[]{:S(2)}) async-start(), calls=%async_computation.3 | async-start | bytes 8847360 | tf_op jit(solution)/shard_map/reduce_scatter | solution.py:97
  127.4 0.8 copy-start.1
  136.2 8.3 %collective-permute-start.2 = (bf16[1,1,16,16,512]{4,3,2,1,0:T(8,128)(2,1)S(1)}, bf16[1,1,16,16,512]{4,3,2,1,0:T(8,128)(2,1)S(1)}, u32[]{:S(2)}, u32[]{:S(2)}) collective-permute-start(bf16[1,1,16,16,512]{4,3,2,1,0:T(8,128)(2,1)S(1)} %get-tuple-element.3), channel_id=1, source_target_pairs={{0,2},{1,3},{4,6},{5,7},{8,10},{9,11},{12,14},{13,15},{16,18},{17,... | collective-permute-start | bytes 786440 | tf_op jit(solution)/shard_map/ppermute | solution.py:18
  137.5 8.4 %collective-permute-start.3 = (bf16[1,1,16,16,512]{4,3,2,1,0:T(8,128)(2,1)S(1)}, bf16[1,1,16,16,512]{4,3,2,1,0:T(8,128)(2,1)S(1)}, u32[]{:S(2)}, u32[]{:S(2)}) collective-permute-start(bf16[1,1,16,16,512]{4,3,2,1,0:T(8,128)(2,1)S(1)} %get-tuple-element.4), channel_id=1, source_target_pairs={{2,0},{3,1},{6,4},{7,5},{10,8},{11,9},{14,12},{15,13},{18,16},{19,... | collective-permute-start | bytes 786440 | tf_op jit(solution)/shard_map/ppermute | solution.py:19
Sparse Core Ops, SparseCore 0:
  84.6 26.5 reduce-scatter.2
  135.2 64.2 reduce-scatter.4
where the time goes:
time: 213 us; the launch traced here: 209 us
  waiting for transfers between devices  74.8 us (35%)
  local copies, waits for them, and re-layouts  65.8 us (31%)
  matrix products  18.1 us (8%)
  between operations  14.5 us (7%)
  blocking collectives  14.4 us (7%)
  starting transfers between devices  13 us (6%)
  other arithmetic  8.65 us (4%)
    reshape x27, local copies, waits for them, and re-layouts, local(): tap_slice(bordered, a, b, c, width_x, width_y, width_z)  44.9 us
    reduce_scatter x1, waiting for transfers between devices, local(): lax.psum_scatter(weight_partial, ('space', 'dp'), scatter_dimension=2, ti...  44.2 us
    reduce_scatter x1, waiting for transfers between devices, local(): lax.psum_scatter(lax.dot_general(flat_weights, stacked, (((0,), (1,)), ((...  26.7 us
    unnamed x62, local copies, waits for them, and re-layouts  15.8 us
    all_gather x1, blocking collectives, local(): grad_full = lax.all_gather(grad_pre, 'chan', axis=4, tiled=True)  14.4 us
    ppermute x2, starting transfers between devices, extended(): after = lax.ppermute(leading, axis, down)  10.4 us
    dot_general x1, matrix products, local(): lax.dot_general(framed_all.reshape(-1, outputs_all), flat_weights, (((1,)...  8.21 us
    dot_general x1, matrix products, local(): lax.dot_general(stacked, interior, (((0,), (0,)), ((), ())), preferred_el...  6.87 us
  transfers between devices with their start and end apart: 6, of which 4 were waited for; matrix products, arithmetic and copies ran while one was open for 6% of the time, Pallas kernels for 0%

commit v1 on v0

--- a/solution.py
+++ b/solution.py
@@ -1,8 +1,11 @@
+import functools
 import math
 
 import jax
 import jax.numpy as jnp
 from jax import lax
+from jax.experimental import pallas as pl
+from jax.experimental.pallas import tpu as pltpu
 from jax.sharding import PartitionSpec as P
 
 tap_offsets = [(a, b, c) for a in (-1, 0, 1) for b in (-1, 0, 1) for c in (-1, 0, 1)]
@@ -29,7 +32,7 @@
     return volume[:, 1 + a : 1 + a + width_x, 1 + b : 1 + b + width_y, 1 + c : 1 + c + width_z]
 
 
-def local(inputs, weights, bias, upstream):
+def local_plain(inputs, weights, bias, upstream):
     batch_size, width_x, width_y, width_z, group_width = inputs.shape
     voxels = batch_size * width_x * width_y * width_z
     tap_count = weights.shape[0]
@@ -100,6 +103,315 @@
     return (activated, grad_inputs, grad_weights)
 
 
+MESH = pl.DeviceIdType.MESH
+LANES = 128
+
+
+def z_shifted(plane):
+    width_y, width_z, lanes = plane.shape
+    rows = width_y * width_z
+    flat = plane.reshape(rows, lanes)
+    wide = flat.astype(jnp.float32)
+    z = lax.broadcasted_iota(jnp.int32, (rows, lanes), 0) % width_z
+    low = jnp.where(z == 0, 0.0, pltpu.roll(wide, 1, 0)).astype(flat.dtype)
+    high = jnp.where(z == width_z - 1, 0.0, pltpu.roll(wide, rows - 1, 0)).astype(flat.dtype)
+    return jnp.concatenate([low, flat, high], axis=1)
+
+
+def z_combined(triple, width_z):
+    rows = triple.shape[0]
+    z = lax.broadcasted_iota(jnp.int32, (rows, LANES), 0) % width_z
+    from_low = pltpu.roll(triple[:, :LANES], rows - 1, 0)
+    from_high = pltpu.roll(triple[:, 2 * LANES :], 1, 0)
+    return (
+        triple[:, LANES : 2 * LANES]
+        + jnp.where(z == width_z - 1, 0.0, from_low)
+        + jnp.where(z == 0, 0.0, from_high)
+    )
+
+
+def fused_kernel(
+    chans, scale,
+    x_ref, w_hbm, b_ref, u_ref,
+    act_ref, gi_ref, gw_ref,
+    w, xa, x3, h3, xt, acc, pb, rb, gpf, gpq, gi32, hs, hr,
+    w_sem, xa_send, xa_recv, rs_send, rs_recv, ag_send, ag_recv, gq_send, gq_recv, hb_send, hb_recv,
+):
+    g, c = lax.axis_index("groups"), lax.axis_index("chan")
+    s, d = lax.axis_index("space"), lax.axis_index("dp")
+    o = 1 - s
+    mine = 2 * s + d
+    width_y, width_z = x_ref.shape[1], x_ref.shape[2]
+    area = width_y * width_z
+    order = (s, o)
+
+    def partner(j):
+        return (o if j >= 2 else s), ((1 - d) if j % 2 else d)
+
+    def far(r):
+        return lax.rem(c + r, chans), lax.rem(c + chans - r, chans)
+
+    weight_copy = pltpu.make_async_copy(w_hbm, w, w_sem)
+    weight_copy.start()
+    barrier = pltpu.get_barrier_semaphore()
+    for j in (1, 2, 3):
+        ps, pd = partner(j)
+        pl.semaphore_signal(barrier, inc=1, device_id=(g, c, ps, pd), device_id_type=MESH)
+    for r in range(1, chans):
+        pl.semaphore_signal(barrier, inc=1, device_id=(g, far(r)[0], s, d), device_id_type=MESH)
+    pl.semaphore_wait(barrier, 3 + chans - 1)
+
+    def x_copy(index, j, plane):
+        ps, pd = partner(j)
+        return pltpu.make_async_remote_copy(
+            src_ref=x_ref.at[plane], dst_ref=xa.at[d, 2 * s + plane],
+            send_sem=xa_send.at[index], recv_sem=xa_recv.at[index],
+            device_id=(g, c, ps, pd), device_id_type=MESH)
+
+    x_list = [(0, 2, o), (1, 2, s), (2, 1, 0), (3, 1, 1), (4, 3, 0), (5, 3, 1)]
+    x_copies = [x_copy(*item) for item in x_list]
+    for copy in x_copies:
+        copy.start()
+
+    def x_arrived(index, j, plane):
+        ps, pd = partner(j)
+        there = {0: s, 1: o}.get(index, plane)
+        pltpu.make_async_remote_copy(
+            src_ref=x_ref.at[there], dst_ref=xa.at[pd, 2 * ps + there],
+            send_sem=xa_send.at[index], recv_sem=xa_recv.at[index],
+            device_id=(g, c, ps, pd), device_id_type=MESH).wait_recv()
+        return pd, 2 * ps + there
+
+    for ref in (x3, gpf):
+        lead = ref.shape[0] * ref.shape[1] if len(ref.shape) == 5 else ref.shape[0]
+        blank = jnp.zeros((width_z, ref.shape[-1]), ref.dtype)
+        for i in range(lead):
+            at = (i // ref.shape[1], i % ref.shape[1]) if len(ref.shape) == 5 else (i,)
+            ref[at + (0,)] = blank
+            ref[at + (width_y + 1,)] = blank
+    h3[0] = jnp.zeros(h3.shape[1:], h3.dtype)
+    h3[width_y + 1] = jnp.zeros(h3.shape[1:], h3.dtype)
+    planes = gpq.shape[1] - 2
+    for crop in range(gpq.shape[0]):
+        for edge in (0, planes + 1):
+            gpq[crop, edge] = jnp.zeros(gpq.shape[2:], gpq.dtype)
+        for plane in range(planes):
+            gpq[crop, plane + 1, 0] = jnp.zeros(gpq.shape[3:], gpq.dtype)
+            gpq[crop, plane + 1, width_y + 1] = jnp.zeros(gpq.shape[3:], gpq.dtype)
+
+    def keep_columns(crop, plane, triple):
+        xt[crop * planes + plane] = triple.T
+
+    triples = []
+    for p in (0, 1):
+        triple = z_shifted(x_ref[p])
+        x3[p, pl.ds(1, width_y)] = triple.reshape(width_y, width_z, 3 * LANES)
+        triples.append(triple)
+
+    def taps_of(a, b):
+        return pl.ds(9 * (a + 1) + 3 * (b + 1), 3)
+
+    def rows_of(ref, b):
+        return ref[pl.ds(1 + b, width_y)].reshape(area, -1)
+
+    def partial_out(sources):
+        left = jnp.concatenate([rows_of(ref, b) for ref, a in sources for b in (-1, 0, 1)], axis=1)
+        right = jnp.concatenate(
+            [w[taps_of(a, b)].reshape(3 * LANES, -1) for ref, a in sources for b in (-1, 0, 1)], axis=0)
+        return jnp.dot(left, right, preferred_element_type=jnp.float32)
+
+    def rs_copy(r, ph):
+        return pltpu.make_async_remote_copy(
+            src_ref=pb.at[ph, far(r)[0]], dst_ref=rb.at[ph, r - 1],
+            send_sem=rs_send.at[r - 1, ph], recv_sem=rs_recv.at[r - 1, ph],
+            device_id=(g, far(r)[0], s, d), device_id_type=MESH)
+
+    def forward(ph, sources):
+        total = partial_out(sources)
+        for t in range(chans):
+            part = total[:, t * LANES : (t + 1) * LANES]
+            acc[ph, t] = part
+            pb[ph, t] = part.astype(pb.dtype)
+        for r in range(1, chans):
+            rs_copy(r, ph).start()
+
+    weight_copy.wait()
+    lean = 1 - 2 * s
+    forward(0, [(x3.at[s], 0), (x3.at[o], lean)])
+    at = x_arrived(*x_list[0])
+    halo = z_shifted(xa[at])
+    h3[pl.ds(1, width_y)] = halo.reshape(width_y, width_z, 3 * LANES)
+    forward(1, [(x3.at[o], 0), (x3.at[s], -lean), (h3, lean)])
+    keep_columns(*at, halo)
+    for p in (0, 1):
+        keep_columns(d, 2 * s + p, triples[p])
+    for item in x_list[1:]:
+        at = x_arrived(*item)
+        keep_columns(*at, z_shifted(xa[at]))
+
+    def ag_copy(r, ph):
+        block = gpf.at[c, order[ph], pl.ds(1, width_y)]
+        return pltpu.make_async_remote_copy(
+            src_ref=block, dst_ref=block,
+            send_sem=ag_send.at[r - 1, ph], recv_sem=ag_recv.at[r - 1, ph],
+            device_id=(g, far(r)[0], s, d), device_id_type=MESH)
+
+    def ag_arrived(r, ph):
+        block = gpf.at[far(r)[1], order[ph], pl.ds(1, width_y)]
+        pltpu.make_async_remote_copy(
+            src_ref=block, dst_ref=block,
+            send_sem=ag_send.at[r - 1, ph], recv_sem=ag_recv.at[r - 1, ph],
+            device_id=(g, far(r)[0], s, d), device_id_type=MESH).wait_recv()
+
+    for ph in (0, 1):
+        plane = order[ph]
+        preact = acc[ph, c] + b_ref[...]
+        for r in range(1, chans):
+            rs_copy(r, ph).wait_recv()
+            preact = preact + rb[ph, r - 1].astype(jnp.float32)
+        gate = jax.nn.sigmoid(preact)
+        act_ref[plane] = (preact * gate).astype(act_ref.dtype).reshape(width_y, width_z, LANES)
+        up = u_ref[plane].reshape(area, LANES).astype(jnp.float32)
+        grad = up * gate * (1.0 + preact * (1.0 - gate))
+        gpf[c, plane, pl.ds(1, width_y)] = grad.astype(gpf.dtype).reshape(width_y, width_z, LANES)
+        for r in range(1, chans):
+            ag_copy(r, ph).start()
+
+    def gq_copy(t, j, ph, crop, where):
+        return pltpu.make_async_remote_copy(
+            src_ref=gpf.at[t, order[ph], pl.ds(1, width_y)],
+            dst_ref=gpq.at[crop, where, pl.ds(1, width_y)],
+            send_sem=gq_send.at[j - 1, ph], recv_sem=gq_recv.at[j - 1, ph],
+            device_id=(g, c, t // 2, t % 2), device_id_type=MESH)
+
+    for ph in (0, 1):
+        here = 1 + 2 * s + order[ph]
+        for r in range(chans):
+            t = far(r)[1]
+            if r:
+                ag_arrived(r, ph)
+            j = 2 * lax.rem(t // 2 + s, 2) + lax.rem(t % 2 + d, 2)
+
+            @pl.when(t != mine)
+            def _(t=t, j=j, ph=ph, here=here):
+                gq_copy(t, j, ph, d, here).start()
+
+            @pl.when(t == mine)
+            def _(t=t, ph=ph, here=here):
+                gpq[d, here, pl.ds(1, width_y)] = gpf[t, order[ph], pl.ds(1, width_y)]
+
+    def back(sources):
+        left = jnp.concatenate(
+            [gpf[t, plane, pl.ds(1 - b, width_y)].reshape(area, LANES)
+             for plane, a in sources for b in (-1, 0, 1) for t in range(chans)], axis=1)
+        right = jnp.concatenate(
+            [w[taps_of(a, b)].reshape(3 * LANES, -1) for plane, a in sources for b in (-1, 0, 1)], axis=1)
+        triple = lax.dot_general(
+            left, right, (((1,), (1,)), ((), ())), preferred_element_type=jnp.float32)
+        return z_combined(triple, width_z)
+
+    hs[...] = back([(o, lean)]).astype(hs.dtype)
+    edge = pltpu.make_async_remote_copy(
+        src_ref=hs, dst_ref=hr, send_sem=hb_send, recv_sem=hb_recv,
+        device_id=(g, c, o, d), device_id_type=MESH)
+    edge.start()
+    gi_ref[s] = back([(s, 0), (o, -lean)]).astype(gi_ref.dtype).reshape(width_y, width_z, LANES)
+    gi32[...] = back([(o, 0), (s, lean)])
+
+    for ph in (0, 1):
+        for j in (1, 2, 3):
+            ps, pd = partner(j)
+            there = ps if ph == 0 else 1 - ps
+            gq_copy(2 * ps + pd, j, ph, pd, 1 + 2 * ps + there).wait_recv()
+
+    def weight_step(step, carry):
+        a, b = step // 3 - 1, step % 3 - 1
+        left = jnp.concatenate([xt[i] for i in range(xt.shape[0])], axis=1)
+        right = gpq[:, pl.ds(1 - a, planes), pl.ds(1 - b, width_y)].reshape(-1, LANES)
+        product = jnp.dot(left, right, preferred_element_type=jnp.float32)
+        gw_ref[pl.ds(3 * step, 3)] = (product * scale).reshape(3, LANES, LANES)
+        return carry
+
+    lax.fori_loop(0, 9, weight_step, 0)
+
+    edge.wait_recv()
+    gi_ref[o] = (gi32[...] + hr[...].astype(jnp.float32)).astype(gi_ref.dtype).reshape(
+        width_y, width_z, LANES)
+
+    edge.wait_send()
+    for copy in x_copies:
+        copy.wait_send()
+    for ph in (0, 1):
+        for r in range(1, chans):
+            rs_copy(r, ph).wait_send()
+            ag_copy(r, ph).wait_send()
+        for j in (1, 2, 3):
+            ps, pd = partner(j)
+            gq_copy(2 * ps + pd, j, ph, d, 1 + 2 * s + order[ph]).wait_send()
+
+
+def local_fused(inputs, weights, bias, upstream):
+    _, width_x, width_y, width_z, lanes = inputs.shape
+    tap_count, _, outputs_all = weights.shape
+    chans, crops = lax.axis_size("chan"), lax.axis_size("dp")
+    planes = width_x * lax.axis_size("space")
+    area = width_y * width_z
+    half, full = jnp.bfloat16, jnp.float32
+    slab = (width_x, width_y, width_z, lanes)
+    dma = pltpu.SemaphoreType.DMA
+    vmem = pl.BlockSpec(memory_space=pltpu.VMEM)
+    flops = 3 * 2 * width_x * area * tap_count * lanes * outputs_all
+    activated, grad_inputs, grad_weights = pl.pallas_call(
+        functools.partial(fused_kernel, chans, 1.0 / math.sqrt(crops * planes * area)),
+        out_shape=[
+            jax.ShapeDtypeStruct(slab, half),
+            jax.ShapeDtypeStruct(slab, half),
+            jax.ShapeDtypeStruct((tap_count, lanes, lanes), full),
+        ],
+        in_specs=[vmem, pl.BlockSpec(memory_space=pl.ANY), vmem, vmem],
+        out_specs=[vmem] * 3,
+        scratch_shapes=[
+            pltpu.VMEM(weights.shape, half),
+            pltpu.VMEM((crops, planes, width_y, width_z, lanes), half),
+            pltpu.VMEM((width_x, width_y + 2, width_z, 3 * lanes), half),
+            pltpu.VMEM((width_y + 2, width_z, 3 * lanes), half),
+            pltpu.VMEM((crops * planes, 3 * lanes, area), half),
+            pltpu.VMEM((2, chans, area, lanes), full),
+            pltpu.VMEM((2, chans, area, lanes), half),
+            pltpu.VMEM((2, chans - 1, area, lanes), half),
+            pltpu.VMEM((chans, width_x, width_y + 2, width_z, lanes), half),
+            pltpu.VMEM((crops, planes + 2, width_y + 2, width_z, lanes), half),
+            pltpu.VMEM((area, lanes), full),
+            pltpu.VMEM((area, lanes), half),
+            pltpu.VMEM((area, lanes), half),
+            dma, dma((6,)), dma((6,)),
+            dma((chans - 1, 2)), dma((chans - 1, 2)),
+            dma((chans - 1, 2)), dma((chans - 1, 2)),
+            dma((3, 2)), dma((3, 2)), dma, dma,
+        ],
+        compiler_params=pltpu.CompilerParams(
+            collective_id=0, has_side_effects=True, vmem_limit_bytes=48 * 1024 * 1024),
+        cost_estimate=pl.CostEstimate(
+            flops=flops, bytes_accessed=2 * weights.size + 4 * tap_count * lanes * lanes,
+            transcendentals=width_x * area * lanes),
+    )(inputs.reshape(slab), weights, bias.reshape(1, lanes), upstream.reshape(slab))
+    return activated[None], grad_inputs[None], grad_weights
+
+
+def local(inputs, weights, bias, upstream):
+    fits = (
+        inputs.shape[0] == 1
+        and inputs.shape[1] == 2
+        and inputs.shape[3] % 16 == 0
+        and inputs.shape[4] == upstream.shape[4] == LANES
+        and weights.shape[2] == LANES * lax.axis_size("chan")
+        and lax.axis_size("chan") == 4
+        and lax.axis_size("space") == 2
+        and lax.axis_size("dp") == 2
+    )
+    return (local_fused if fits else local_plain)(inputs, weights, bias, upstream)
+
+
 def solution(mesh):
     return jax.shard_map(
         local,

time: 213 us -> 46.7 us (0.22)
  the two profiles are of different devices: /device:TPU:26 before, /device:TPU:1 now
where the time goes in v1:
time: 46.7 us; the launch traced here: 46.5 us
  Pallas kernels  38.9 us (83%)
  local copies, waits for them, and re-layouts  6.98 us (15%)
  between operations  0.65 us (1%)
    pallas_call x1, Pallas kernels, local_fused(): pl.pallas_call(functools.partial(fused_kernel, chans, 1.0 / math.sqrt(cro...  38.9 us
    unnamed x11, local copies, waits for them, and re-layouts  6.98 us

profile of v1, /device:TPU:1, one launch (start us, length us, event | category | flops | bytes accessed | tf_op | source)
XLA Modules:
  0.0 46.5 jit_solution(11599913923156524409)
XLA Ops:
  0.6 0.0 copy-start
  0.6 2.0 %copy-done = bf16[27,128,512]{2,1,0:T(8,128)(2,1)S(1)} copy-done((bf16[27,128,512]{2,1,0:T(8,128)(2,1)S(1)}, bf16[27,128,512]{2,1,0:T(8,128)(2,1)}, u32[]{:S(2)}) %copy-start) | copy-done | bytes 3538968
  2.6 0.0 copy-start.1
  2.6 0.9 %copy-done.1 = bf16[1,2,16,16,128]{4,3,2,1,0:T(8,128)(2,1)S(1)} copy-done((bf16[1,2,16,16,128]{4,3,2,1,0:T(8,128)(2,1)S(1)}, bf16[1,2,16,16,128]{4,3,2,1,0:T(8,128)(2,1)}, u32[]{:S(2)}) %copy-start.1) | copy-done | bytes 131096
  3.5 0.0 copy-start.2
  3.5 0.9 %copy-done.2 = bf16[1,2,16,16,128]{4,3,2,1,0:T(8,128)(2,1)S(1)} copy-done((bf16[1,2,16,16,128]{4,3,2,1,0:T(8,128)(2,1)S(1)}, bf16[1,2,16,16,128]{4,3,2,1,0:T(8,128)(2,1)}, u32[]{:S(2)}) %copy-start.2) | copy-done | bytes 131096
  4.4 0.0 copy-start.3
  4.4 0.7 %copy-done.3 = f32[128]{0:T(128)S(1)} copy-done((f32[128]{0:T(128)S(1)}, f32[128]{0:T(128)}, u32[]{:S(2)}) %copy-start.3) | copy-done | bytes 536
  5.1 38.9 %shard_map.67 = (bf16[2,16,16,128]{3,2,1,0:T(8,128)(2,1)S(1)}, bf16[2,16,16,128]{3,2,1,0:T(8,128)(2,1)S(1)}, f32[27,128,128]{2,1,0:T(8,128)S(1)}) custom-call(bf16[2,16,16,128]{3,2,1,0:T(8,128)(2,1)S(1)} %bitcast.7, bf16[27,128,512]{2,1,0:T(8,128)(2,1)S(1)} %copy-done, f32[1,128]{1,0:T(1,128)S(1)} %bitcast.9, bf16[2,16,16,128]{3,2,1,0:T(8,128)(2,1)S(1)} %bitcast.8), custom_call_target="tpu_custom_call" | custom-call | flops 5435817984 | bytes 5308416 | tf_op jit(solution)/shard_map/pallas_call | solution.py:364
  44.0 0.7 %copy.10 = bf16[1,2,16,16,128]{4,3,2,1,0:T(8,128)(2,1)} copy(bf16[1,2,16,16,128]{4,3,2,1,0:T(8,128)(2,1)S(1)} %bitcast.6) | data formatting | bytes 262144
  44.7 0.7 %copy.11 = bf16[1,2,16,16,128]{4,3,2,1,0:T(8,128)(2,1)} copy(bf16[1,2,16,16,128]{4,3,2,1,0:T(8,128)(2,1)S(1)} %bitcast.5) | data formatting | bytes 262144
  45.3 1.2 %copy.12 = f32[27,128,128]{2,1,0:T(8,128)} copy(f32[27,128,128]{2,1,0:T(8,128)S(1)} %get-tuple-element.14) | data formatting | bytes 3538944
Async XLA Ops:
  0.6 2.0 %copy-start = (bf16[27,128,512]{2,1,0:T(8,128)(2,1)S(1)}, bf16[27,128,512]{2,1,0:T(8,128)(2,1)}, u32[]{:S(2)}) copy-start(bf16[27,128,512]{2,1,0:T(8,128)(2,1)} %w_hbm.1) | copy-start | bytes 10616836
  2.6 0.9 %copy-start.1 = (bf16[1,2,16,16,128]{4,3,2,1,0:T(8,128)(2,1)S(1)}, bf16[1,2,16,16,128]{4,3,2,1,0:T(8,128)(2,1)}, u32[]{:S(2)}) copy-start(bf16[1,2,16,16,128]{4,3,2,1,0:T(8,128)(2,1)} %param.4) | copy-start | bytes 393220
  3.5 0.9 %copy-start.2 = (bf16[1,2,16,16,128]{4,3,2,1,0:T(8,128)(2,1)S(1)}, bf16[1,2,16,16,128]{4,3,2,1,0:T(8,128)(2,1)}, u32[]{:S(2)}) copy-start(bf16[1,2,16,16,128]{4,3,2,1,0:T(8,128)(2,1)} %param.7) | copy-start | bytes 393220
  4.4 0.7 %copy-start.3 = (f32[128]{0:T(128)S(1)}, f32[128]{0:T(128)}, u32[]{:S(2)}) copy-start(f32[128]{0:T(128)} %param.6) | copy-start | bytes 1540

commit v2 on v1

--- a/solution.py
+++ b/solution.py
@@ -132,10 +132,10 @@
 
 def fused_kernel(
     chans, scale,
-    x_ref, w_hbm, b_ref, u_ref,
+    x_hbm, w_hbm, b_hbm, u_hbm,
     act_ref, gi_ref, gw_ref,
-    w, xa, x3, h3, xt, acc, pb, rb, gpf, gpq, gi32, hs, hr,
-    w_sem, xa_send, xa_recv, rs_send, rs_recv, ag_send, ag_recv, gq_send, gq_recv, hb_send, hb_recv,
+    x_ref, b_ref, u_ref, w, xa, x3, h3, xt, acc, pb, rb, gpf, gpq, gi32, hs, hr,
+    in_sem, xa_send, xa_recv, rs_send, rs_recv, ag_send, ag_recv, gq_send, gq_recv, hb_send, hb_recv,
 ):
     g, c = lax.axis_index("groups"), lax.axis_index("chan")
     s, d = lax.axis_index("space"), lax.axis_index("dp")
@@ -151,57 +151,51 @@
     def far(r):
         return lax.rem(c + r, chans), lax.rem(c + chans - r, chans)
 
-    weight_copy = pltpu.make_async_copy(w_hbm, w, w_sem)
-    weight_copy.start()
+    loads = [
+        pltpu.make_async_copy(source, target, in_sem.at[i])
+        for i, (source, target) in enumerate(
+            ((x_hbm, x_ref), (w_hbm, w), (b_hbm, b_ref), (u_hbm, u_ref)))
+    ]
+    for load in loads:
+        load.start()
     barrier = pltpu.get_barrier_semaphore()
     for j in (1, 2, 3):
         ps, pd = partner(j)
         pl.semaphore_signal(barrier, inc=1, device_id=(g, c, ps, pd), device_id_type=MESH)
     for r in range(1, chans):
         pl.semaphore_signal(barrier, inc=1, device_id=(g, far(r)[0], s, d), device_id_type=MESH)
-    pl.semaphore_wait(barrier, 3 + chans - 1)
 
     def x_copy(index, j, plane):
         ps, pd = partner(j)
         return pltpu.make_async_remote_copy(
-            src_ref=x_ref.at[plane], dst_ref=xa.at[d, 2 * s + plane],
+            src_ref=x_hbm.at[plane], dst_ref=xa.at[d, 2 * s + plane],
             send_sem=xa_send.at[index], recv_sem=xa_recv.at[index],
             device_id=(g, c, ps, pd), device_id_type=MESH)
 
     x_list = [(0, 2, o), (1, 2, s), (2, 1, 0), (3, 1, 1), (4, 3, 0), (5, 3, 1)]
     x_copies = [x_copy(*item) for item in x_list]
-    for copy in x_copies:
-        copy.start()
 
     def x_arrived(index, j, plane):
         ps, pd = partner(j)
         there = {0: s, 1: o}.get(index, plane)
         pltpu.make_async_remote_copy(
-            src_ref=x_ref.at[there], dst_ref=xa.at[pd, 2 * ps + there],
+            src_ref=x_hbm.at[there], dst_ref=xa.at[pd, 2 * ps + there],
             send_sem=xa_send.at[index], recv_sem=xa_recv.at[index],
             device_id=(g, c, ps, pd), device_id_type=MESH).wait_recv()
         return pd, 2 * ps + there
 
-    for ref in (x3, gpf):
-        lead = ref.shape[0] * ref.shape[1] if len(ref.shape) == 5 else ref.shape[0]
-        blank = jnp.zeros((width_z, ref.shape[-1]), ref.dtype)
-        for i in range(lead):
-            at = (i // ref.shape[1], i % ref.shape[1]) if len(ref.shape) == 5 else (i,)
-            ref[at + (0,)] = blank
-            ref[at + (width_y + 1,)] = blank
-    h3[0] = jnp.zeros(h3.shape[1:], h3.dtype)
-    h3[width_y + 1] = jnp.zeros(h3.shape[1:], h3.dtype)
-    planes = gpq.shape[1] - 2
-    for crop in range(gpq.shape[0]):
-        for edge in (0, planes + 1):
-            gpq[crop, edge] = jnp.zeros(gpq.shape[2:], gpq.dtype)
-        for plane in range(planes):
-            gpq[crop, plane + 1, 0] = jnp.zeros(gpq.shape[3:], gpq.dtype)
-            gpq[crop, plane + 1, width_y + 1] = jnp.zeros(gpq.shape[3:], gpq.dtype)
+    def blank_rows(ref, at):
+        blank = jnp.zeros(ref.shape[-2:], ref.dtype)
+        ref[at + (0,)] = blank
+        ref[at + (width_y + 1,)] = blank
+
+    for p in (0, 1):
+        blank_rows(x3, (p,))
 
     def keep_columns(crop, plane, triple):
-        xt[crop * planes + plane] = triple.T
-
+        xt[crop * gpq.shape[1] + plane] = triple.T
+
+    loads[0].wait()
     triples = []
     for p in (0, 1):
         triple = z_shifted(x_ref[p])
@@ -232,16 +226,31 @@
             part = total[:, t * LANES : (t + 1) * LANES]
             acc[ph, t] = part
             pb[ph, t] = part.astype(pb.dtype)
+
+    def scatter(ph):
         for r in range(1, chans):
             rs_copy(r, ph).start()
 
-    weight_copy.wait()
+    loads[1].wait()
     lean = 1 - 2 * s
     forward(0, [(x3.at[s], 0), (x3.at[o], lean)])
+    pl.semaphore_wait(barrier, 3 + chans - 1)
+    scatter(0)
+    for copy in x_copies:
+        copy.start()
+    blank_rows(h3, ())
+    for t in range(chans):
+        for p in (0, 1):
+            blank_rows(gpf, (t, p))
+    planes = gpq.shape[1]
+    for crop in range(gpq.shape[0]):
+        for p in range(planes):
+            blank_rows(gpq, (crop, p))
     at = x_arrived(*x_list[0])
     halo = z_shifted(xa[at])
     h3[pl.ds(1, width_y)] = halo.reshape(width_y, width_z, 3 * LANES)
     forward(1, [(x3.at[o], 0), (x3.at[s], -lean), (h3, lean)])
+    scatter(1)
     keep_columns(*at, halo)
     for p in (0, 1):
         keep_columns(d, 2 * s + p, triples[p])
@@ -263,6 +272,8 @@
             send_sem=ag_send.at[r - 1, ph], recv_sem=ag_recv.at[r - 1, ph],
             device_id=(g, far(r)[0], s, d), device_id_type=MESH).wait_recv()
 
+    loads[2].wait()
+    loads[3].wait()
     for ph in (0, 1):
         plane = order[ph]
         preact = acc[ph, c] + b_ref[...]
@@ -284,8 +295,8 @@
             send_sem=gq_send.at[j - 1, ph], recv_sem=gq_recv.at[j - 1, ph],
             device_id=(g, c, t // 2, t % 2), device_id_type=MESH)
 
-    for ph in (0, 1):
-        here = 1 + 2 * s + order[ph]
+    def spread(ph):
+        here = 2 * s + order[ph]
         for r in range(chans):
             t = far(r)[1]
             if r:
@@ -293,49 +304,66 @@
             j = 2 * lax.rem(t // 2 + s, 2) + lax.rem(t % 2 + d, 2)
 
             @pl.when(t != mine)
-            def _(t=t, j=j, ph=ph, here=here):
+            def _(t=t, j=j):
                 gq_copy(t, j, ph, d, here).start()
 
             @pl.when(t == mine)
-            def _(t=t, ph=ph, here=here):
+            def _(t=t):
                 gpq[d, here, pl.ds(1, width_y)] = gpf[t, order[ph], pl.ds(1, width_y)]
 
-    def back(sources):
+    def back(plane, a):
         left = jnp.concatenate(
             [gpf[t, plane, pl.ds(1 - b, width_y)].reshape(area, LANES)
-             for plane, a in sources for b in (-1, 0, 1) for t in range(chans)], axis=1)
+             for b in (-1, 0, 1) for t in range(chans)], axis=1)
         right = jnp.concatenate(
-            [w[taps_of(a, b)].reshape(3 * LANES, -1) for plane, a in sources for b in (-1, 0, 1)], axis=1)
+            [w[taps_of(a, b)].reshape(3 * LANES, -1) for b in (-1, 0, 1)], axis=1)
         triple = lax.dot_general(
             left, right, (((1,), (1,)), ((), ())), preferred_element_type=jnp.float32)
         return z_combined(triple, width_z)
 
-    hs[...] = back([(o, lean)]).astype(hs.dtype)
+    def collected(ph):
+        for j in (1, 2, 3):
+            ps, pd = partner(j)
+            there = ps if ph == 0 else 1 - ps
+            gq_copy(2 * ps + pd, j, ph, pd, 2 * ps + there).wait_recv()
+
+    def weight_part(ph):
+        held = (0, 3) if ph == 0 else (1, 2)
+        crops = range(gpq.shape[0])
+
+        def step(i, carry):
+            for a in (-1, 0, 1):
+                pairs = [(crop, v) for crop in crops for v in held if 0 <= v + a < planes]
+                left = jnp.concatenate([xt[crop * planes + v + a] for crop, v in pairs], axis=1)
+                right = jnp.concatenate(
+                    [gpq[crop, v, pl.ds(2 - i, width_y)].reshape(area, LANES) for crop, v in pairs],
+                    axis=0)
+                product = jnp.dot(left, right, preferred_element_type=jnp.float32)
+                product = product.reshape(3, LANES, LANES)
+                at = pl.ds(9 * (a + 1) + 3 * i, 3)
+                gw_ref[at] = product if ph == 0 else (gw_ref[at] + product) * scale
+            return carry
+
+        lax.fori_loop(0, 3, step, 0)
+
+    spread(0)
+    gi32[0] = back(s, 0)
+    gi32[1] = back(s, lean)
+    collected(0)
+    weight_part(0)
+    spread(1)
+    hs[...] = back(o, lean).astype(hs.dtype)
     edge = pltpu.make_async_remote_copy(
         src_ref=hs, dst_ref=hr, send_sem=hb_send, recv_sem=hb_recv,
         device_id=(g, c, o, d), device_id_type=MESH)
     edge.start()
-    gi_ref[s] = back([(s, 0), (o, -lean)]).astype(gi_ref.dtype).reshape(width_y, width_z, LANES)
-    gi32[...] = back([(o, 0), (s, lean)])
-
-    for ph in (0, 1):
-        for j in (1, 2, 3):
-            ps, pd = partner(j)
-            there = ps if ph == 0 else 1 - ps
-            gq_copy(2 * ps + pd, j, ph, pd, 1 + 2 * ps + there).wait_recv()
-
-    def weight_step(step, carry):
-        a, b = step // 3 - 1, step % 3 - 1
-        left = jnp.concatenate([xt[i] for i in range(xt.shape[0])], axis=1)
-        right = gpq[:, pl.ds(1 - a, planes), pl.ds(1 - b, width_y)].reshape(-1, LANES)
-        product = jnp.dot(left, right, preferred_element_type=jnp.float32)
-        gw_ref[pl.ds(3 * step, 3)] = (product * scale).reshape(3, LANES, LANES)
-        return carry
-
-    lax.fori_loop(0, 9, weight_step, 0)
+    gi_ref[s] = (gi32[0] + back(o, -lean)).astype(gi_ref.dtype).reshape(width_y, width_z, LANES)
+    gi32[1] = gi32[1] + back(o, 0)
+    collected(1)
+    weight_part(1)
 
     edge.wait_recv()
-    gi_ref[o] = (gi32[...] + hr[...].astype(jnp.float32)).astype(gi_ref.dtype).reshape(
+    gi_ref[o] = (gi32[1] + hr[...].astype(jnp.float32)).astype(gi_ref.dtype).reshape(
         width_y, width_z, LANES)
 
     edge.wait_send()
@@ -347,7 +375,7 @@
             ag_copy(r, ph).wait_send()
         for j in (1, 2, 3):
             ps, pd = partner(j)
-            gq_copy(2 * ps + pd, j, ph, d, 1 + 2 * s + order[ph]).wait_send()
+            gq_copy(2 * ps + pd, j, ph, d, 2 * s + order[ph]).wait_send()
 
 
 def local_fused(inputs, weights, bias, upstream):
@@ -368,9 +396,12 @@
             jax.ShapeDtypeStruct(slab, half),
             jax.ShapeDtypeStruct((tap_count, lanes, lanes), full),
         ],
-        in_specs=[vmem, pl.BlockSpec(memory_space=pl.ANY), vmem, vmem],
+        in_specs=[pl.BlockSpec(memory_space=pltpu.HBM)] * 4,
         out_specs=[vmem] * 3,
         scratch_shapes=[
+            pltpu.VMEM(slab, half),
+            pltpu.VMEM((1, lanes), full),
+            pltpu.VMEM(slab, half),
             pltpu.VMEM(weights.shape, half),
             pltpu.VMEM((crops, planes, width_y, width_z, lanes), half),
             pltpu.VMEM((width_x, width_y + 2, width_z, 3 * lanes), half),
@@ -380,17 +411,17 @@
             pltpu.VMEM((2, chans, area, lanes), half),
             pltpu.VMEM((2, chans - 1, area, lanes), half),
             pltpu.VMEM((chans, width_x, width_y + 2, width_z, lanes), half),
-            pltpu.VMEM((crops, planes + 2, width_y + 2, width_z, lanes), half),
-            pltpu.VMEM((area, lanes), full),
+            pltpu.VMEM((crops, planes, width_y + 2, width_z, lanes), half),
+            pltpu.VMEM((2, area, lanes), full),
             pltpu.VMEM((area, lanes), half),
             pltpu.VMEM((area, lanes), half),
-            dma, dma((6,)), dma((6,)),
+            dma((4,)), dma((6,)), dma((6,)),
             dma((chans - 1, 2)), dma((chans - 1, 2)),
             dma((chans - 1, 2)), dma((chans - 1, 2)),
             dma((3, 2)), dma((3, 2)), dma, dma,
         ],
         compiler_params=pltpu.CompilerParams(
-            collective_id=0, has_side_effects=True, vmem_limit_bytes=48 * 1024 * 1024),
+            collective_id=0, has_side_effects=True, vmem_limit_bytes=60 * 1024 * 1024),
         cost_estimate=pl.CostEstimate(
             flops=flops, bytes_accessed=2 * weights.size + 4 * tap_count * lanes * lanes,
             transcendentals=width_x * area * lanes),

time: 46.7 us -> 46.2 us (0.989)
  the two profiles are of different devices: /device:TPU:1 before, /device:TPU:26 now
where the time goes in v2:
time: 46.2 us; the launch traced here: 46 us
  Pallas kernels  39.4 us (85%)
  local copies, waits for them, and re-layouts  6.01 us (13%)
  between operations  0.64 us (1%)
    pallas_call x1, Pallas kernels, local_fused(): pl.pallas_call(functools.partial(fused_kernel, chans, 1.0 / math.sqrt(cro...  39.4 us
    unnamed x3, local copies, waits for them, and re-layouts  6.01 us

profile of v2, /device:TPU:26, one launch (start us, length us, event | category | flops | bytes accessed | tf_op | source)
XLA Modules:
  0.0 46.0 jit_solution(5967564770124542511)
XLA Ops:
  0.6 39.4 %shard_map.67 = (bf16[2,16,16,128]{3,2,1,0:T(8,128)(2,1)}, bf16[2,16,16,128]{3,2,1,0:T(8,128)(2,1)}, f32[27,128,128]{2,1,0:T(8,128)}) custom-call(bf16[2,16,16,128]{3,2,1,0:T(8,128)(2,1)} %bitcast.7, bf16[27,128,512]{2,1,0:T(8,128)(2,1)} %w_hbm.1, f32[1,128]{1,0:T(1,128)} %bitcast.9, bf16[2,16,16,128]{3,2,1,0:T(8,128)(2,1)} %bitcast.8), custom_call_target="tpu_custom_call" | custom-call | flops 5435817984 | bytes 5308416 | tf_op jit(solution)/shard_map/pallas_call | solution.py:392
  40.0 1.6 %copy.10 = bf16[1,2,16,16,128]{4,3,2,1,0:T(8,128)(2,1)} copy(bf16[1,2,16,16,128]{4,3,2,1,0:T(8,128)(2,1)} %bitcast.6) | data formatting | bytes 262144
  41.6 1.6 %copy.11 = bf16[1,2,16,16,128]{4,3,2,1,0:T(8,128)(2,1)} copy(bf16[1,2,16,16,128]{4,3,2,1,0:T(8,128)(2,1)} %bitcast.5) | data formatting | bytes 262144
  43.2 2.9 %copy.12 = f32[27,128,128]{2,1,0:T(8,128)} copy(f32[27,128,128]{2,1,0:T(8,128)} %get-tuple-element.14) | data formatting | bytes 3538944

commit v3 on v2

--- a/solution.py
+++ b/solution.py
@@ -131,7 +131,7 @@
 
 
 def fused_kernel(
-    chans, scale,
+    chans,
     x_hbm, w_hbm, b_hbm, u_hbm,
     act_ref, gi_ref, gw_ref,
     x_ref, b_ref, u_ref, w, xa, x3, h3, xt, acc, pb, rb, gpf, gpq, gi32, hs, hr,
@@ -341,7 +341,7 @@
                 product = jnp.dot(left, right, preferred_element_type=jnp.float32)
                 product = product.reshape(3, LANES, LANES)
                 at = pl.ds(9 * (a + 1) + 3 * i, 3)
-                gw_ref[at] = product if ph == 0 else (gw_ref[at] + product) * scale
+                gw_ref[at] = product if ph == 0 else gw_ref[at] + product
             return carry
 
         lax.fori_loop(0, 3, step, 0)
@@ -390,10 +390,10 @@
     vmem = pl.BlockSpec(memory_space=pltpu.VMEM)
     flops = 3 * 2 * width_x * area * tap_count * lanes * outputs_all
     activated, grad_inputs, grad_weights = pl.pallas_call(
-        functools.partial(fused_kernel, chans, 1.0 / math.sqrt(crops * planes * area)),
+        functools.partial(fused_kernel, chans),
         out_shape=[
-            jax.ShapeDtypeStruct(slab, half),
-            jax.ShapeDtypeStruct(slab, half),
+            jax.ShapeDtypeStruct(slab, full),
+            jax.ShapeDtypeStruct(slab, full),
             jax.ShapeDtypeStruct((tap_count, lanes, lanes), full),
         ],
         in_specs=[pl.BlockSpec(memory_space=pltpu.HBM)] * 4,
@@ -426,7 +426,8 @@
             flops=flops, bytes_accessed=2 * weights.size + 4 * tap_count * lanes * lanes,
             transcendentals=width_x * area * lanes),
     )(inputs.reshape(slab), weights, bias.reshape(1, lanes), upstream.reshape(slab))
-    return activated[None], grad_inputs[None], grad_weights
+    scale = 1.0 / math.sqrt(crops * planes * area)
+    return activated[None].astype(half), grad_inputs[None].astype(half), grad_weights * scale
 
 
 def local(inputs, weights, bias, upstream):

time: 46.2 us -> 44.9 us (0.972)
  local copies, waits for them, and re-layouts: 6.01 us -> 0 us
  other arithmetic: 0 us -> 4.69 us
    unnamed x3 -> x0, local copies, waits for them, and re-layouts: 6.01 us -> none
    mul x0 -> x1, other arithmetic: none -> 2.92 us  [local_fused(): grad_weights * scale]
    convert_element_type x0 -> x1, other arithmetic: none -> 1.77 us  [local_fused(): grad_inputs[None].astype(half)]
where the time goes in v3:
time: 44.9 us; the launch traced here: 44.8 us
  Pallas kernels  39.4 us (88%)
  other arithmetic  4.69 us (10%)
  between operations  0.64 us (1%)
    pallas_call x1, Pallas kernels, local_fused(): pl.pallas_call(functools.partial(fused_kernel, chans), out_shape=[jax.Sha...  39.4 us
    mul x1, other arithmetic, local_fused(): grad_weights * scale  2.92 us
    convert_element_type x1, other arithmetic, local_fused(): grad_inputs[None].astype(half)  1.77 us

profile of v3, /device:TPU:26, one launch (start us, length us, event | category | flops | bytes accessed | tf_op | source)
XLA Modules:
  0.0 44.8 jit_solution(9361904044390559172)
XLA Ops:
  0.6 39.4 %shard_map.67 = (f32[2,16,16,128]{3,2,1,0:T(8,128)}, f32[2,16,16,128]{3,2,1,0:T(8,128)}, f32[27,128,128]{2,1,0:T(8,128)}) custom-call(bf16[2,16,16,128]{3,2,1,0:T(8,128)(2,1)} %bitcast.7, bf16[27,128,512]{2,1,0:T(8,128)(2,1)} %w_hbm.1, f32[1,128]{1,0:T(1,128)} %bitcast.9, bf16[2,16,16,128]{3,2,1,0:T(8,128)(2,1)} %bitcast.8), custom_call_target="tpu_custom_call" | custom-call | flops 5435817984 | bytes 5308416 | tf_op jit(solution)/shard_map/pallas_call | solution.py:392
  40.1 1.8 %convert_bitcast_fusion = (bf16[1,2,16,16,128]{4,3,2,1,0:T(8,128)(2,1)}, bf16[1,2,16,16,128]{4,3,2,1,0:T(8,128)(2,1)}) fusion(f32[2,16,16,128]{3,2,1,0:T(8,128)} %get-tuple-element.7, f32[2,16,16,128]{3,2,1,0:T(8,128)} %get-tuple-element.6), kind=kLoop, calls=%fused_computation.1 | loop fusion | flops 131072 | bytes 786432 | tf_op jit(solution)/shard_map/convert_element_type | solution.py:430
  41.8 2.9 %broadcast_multiply_fusion = f32[27,128,128]{2,1,0:T(8,128)} fusion(f32[27,128,128]{2,1,0:T(8,128)} %get-tuple-element.8), kind=kLoop, calls=%fused_computation | loop fusion | flops 442368 | bytes 3538944 | tf_op jit(solution)/shard_map/mul | solution.py:430
